TPU v7x, 32 devices: a whole 2x2x4 slice. The times are simulated.
32 devices in a mesh: dp: 4 (over z), seq: 8 (over y, x, core).
Axes of the slice: x: 2, y: 2, z: 4, core: 2. Of those that a mesh axis runs over, the one named last changes fastest.
Arguments:
- inputs: bfloat16 [16, 2048, 896], P('dp', 'seq'), may hold values from -6 to 6
- cotangent: bfloat16 [16, 2048, 896], P('dp', 'seq'), may hold values from -6 to 6
- segments: int32 [16, 2048], P('dp', 'seq'), may hold values from 0 to 10, as said below
- positions: int32 [16, 2048], P('dp', 'seq'), may hold values from 0 to 3998, as said below
- attn_master: float32 [1838080], P('seq')
- attn_moment: float32 [1838080], P('seq'), may hold values from -0.3 to 0.3
- attn_second: float32 [1838080], P('seq'), may hold values from 0.001 to 0.1
- ffn_master: float32 [13074432], P('seq')
- ffn_moment: float32 [13074432], P('seq'), may hold values from -0.3 to 0.3
- ffn_second: float32 [13074432], P('seq'), may hold values from 0.001 to 0.1
Outputs:
- result: bfloat16 [16, 2048, 896], P('dp', 'seq')
- grad_input: float32 [16, 2048, 896], P('dp', 'seq')
- attn_change: float32 [1838080], P('seq')
- moment_attn: float32 [1838080], P('seq')
- second_attn: float32 [1838080], P('seq')
- grad_attn: float32 [1838080], P('seq')
- ffn_change: float32 [13074432], P('seq')
- moment_ffn: float32 [13074432], P('seq')
- second_ffn: float32 [13074432], P('seq')
- grad_ffn: float32 [13074432], P('seq')
Inputs may be any that keep to these rules, and one draw needn't show every extreme that they name: `segments`: in each sequence the document number starts at 0 and rises by one where a new document begins; every document has 200 to 2000 tokens, except the last of a sequence, which may be cut shorter. `positions`: A token's position is its index within its document plus an offset of 0 to 1999 drawn for each document.
All inputs are finite; a program needn't handle non-finite values.
Results may differ from a plain program's by a relative error of at most 0.025.
Values may be sent and summed in bfloat16 or wider, within the bound.
A program may use at most 640 MiB of HBM per device.

v0:
```python
import math
import jax
import jax.numpy as jnp
from jax import lax
from jax.sharding import PartitionSpec as P

D = 896
H = 14
KV = 2
HD = 64
FF = 4864
STEP = 8
norm_eps = 1e-06
rope_base = 1000000.0
first_decay = 0.9
second_decay = 0.95
learn_rate = 0.01
weight_decay = 0.1
adam_eps = 1e-08
masked_score = -1e30


def split_weights(attn_flat, ffn_flat):
    kv_width = KV * HD
    qkv_width = D + 2 * kv_width
    offset = 2 * D + qkv_width
    gain_one = attn_flat[0:D].astype(jnp.float32)
    gain_two = attn_flat[D : 2 * D].astype(jnp.float32)
    bias_qkv = attn_flat[2 * D : offset].astype(jnp.float32)
    w_qkv = attn_flat[offset : offset + D * qkv_width].reshape(D, qkv_width)
    w_out = attn_flat[offset + D * qkv_width : offset + D * qkv_width + D * D].reshape(D, D)
    w_gu = ffn_flat[: 2 * D * FF].reshape(D, 2 * FF)
    w_down = ffn_flat[2 * D * FF :].reshape(FF, D)
    return (gain_one, gain_two, bias_qkv, w_qkv, w_out, w_gu, w_down)


def rope_tables(pos_values):
    halfway = HD // 2
    frequency = jnp.exp(jnp.arange(halfway, dtype=jnp.float32) * (-2.0 * math.log(rope_base) / HD))
    angles = pos_values.astype(jnp.float32)[..., None] * frequency
    return (jnp.cos(angles), jnp.sin(angles))


def rotate(values, cosine, sine_table):
    halfway = values.shape[-1] // 2
    front_half = values[..., :halfway]
    back_half = values[..., halfway:]
    return jnp.concatenate(
        [
            front_half * cosine - back_half * sine_table,
            back_half * cosine + front_half * sine_table,
        ],
        axis=-1,
    )


def rotate_back(gradient, cosine, sine_table):
    halfway = gradient.shape[-1] // 2
    front_half = gradient[..., :halfway]
    back_half = gradient[..., halfway:]
    return jnp.concatenate(
        [
            front_half * cosine + back_half * sine_table,
            back_half * cosine - front_half * sine_table,
        ],
        axis=-1,
    )


def norm_back(values, inverse, gain, grad_norm):
    weighted = grad_norm * gain
    grad_gain = jnp.sum(grad_norm * values * inverse, axis=(0, 1))
    grad_in = inverse * weighted - values * inverse**3 * jnp.mean(
        values * weighted, axis=-1, keepdims=True
    )
    return (grad_in, grad_gain)


def adam_step(master, moment, second, gradient):
    moment_new = first_decay * moment + (1.0 - first_decay) * gradient
    second_new = second_decay * second + (1.0 - second_decay) * gradient * gradient
    corrected = moment_new / (1.0 - first_decay**STEP)
    spread_root = jnp.sqrt(second_new / (1.0 - second_decay**STEP))
    change = -learn_rate * (corrected / (spread_root + adam_eps) + weight_decay * master)
    return (change, moment_new, second_new)


def per_device(
    inputs,
    cotangent,
    segments,
    positions,
    attn_master,
    attn_moment,
    attn_second,
    ffn_master,
    ffn_moment,
    ffn_second,
):
    seq_count = inputs.shape[0]
    local_rows = inputs.shape[1]
    seq_parts = lax.axis_size("seq")
    seq_length = local_rows * seq_parts
    seq_rank = lax.axis_index("seq")
    token_scale = 1.0 / math.sqrt(seq_count * seq_length * lax.axis_size("dp"))
    kv_width = KV * HD
    groups = H // KV
    score_scale = HD ** (-0.5)
    attn_flat, ffn_flat = (
        lax.all_gather(attn_master.astype(jnp.bfloat16), "seq", axis=0, tiled=True),
        lax.all_gather(ffn_master.astype(jnp.bfloat16), "seq", axis=0, tiled=True),
    )
    gain_one, gain_two, bias_qkv, w_qkv, w_out, w_gu, w_down = split_weights(attn_flat, ffn_flat)
    x_wide = inputs.astype(jnp.float32)
    inv_one = lax.rsqrt(jnp.mean(x_wide * x_wide, axis=-1, keepdims=True) + norm_eps)
    normed_one = (x_wide * inv_one * gain_one).astype(jnp.bfloat16)
    qkv_proj = (
        jnp.einsum("scd,de->sce", normed_one, w_qkv, preferred_element_type=jnp.float32) + bias_qkv
    )
    cosine, sine_table = rope_tables(positions)
    cos_query = cosine[:, :, None, None, :]
    sin_query = sine_table[:, :, None, None, :]
    cos_key = cosine[:, :, None, :]
    sin_key = sine_table[:, :, None, :]
    queries = rotate(
        qkv_proj[..., :D].reshape(seq_count, local_rows, KV, groups, HD), cos_query, sin_query
    ).astype(jnp.bfloat16)
    key_rows = rotate(
        qkv_proj[..., D : D + kv_width].reshape(seq_count, local_rows, KV, HD), cos_key, sin_key
    )
    key_rows = key_rows.astype(jnp.bfloat16).reshape(seq_count, local_rows, kv_width)
    value_rows = qkv_proj[..., D + kv_width :].astype(jnp.bfloat16)
    key_all, value_all, seg_all = (
        lax.all_gather(key_rows, "seq", axis=1, tiled=True),
        lax.all_gather(value_rows, "seq", axis=1, tiled=True),
        lax.all_gather(segments.astype(jnp.bfloat16), "seq", axis=1, tiled=True),
    )
    key_span = min(512, seq_length)
    block_count = seq_length // key_span
    query_place = seq_rank * local_rows + jnp.arange(local_rows, dtype=jnp.int32)
    seg_query = segments.astype(jnp.float32)
    nothing = jnp.zeros((), jnp.float32)

    def block_parts(block_index):
        first_key = block_index * key_span
        key_block = key_all[:, first_key : first_key + key_span].reshape(
            seq_count, key_span, KV, HD
        )
        value_block = value_all[:, first_key : first_key + key_span].reshape(
            seq_count, key_span, KV, HD
        )
        key_place = first_key + jnp.arange(key_span, dtype=jnp.int32)
        seg_keys = seg_all[:, first_key : first_key + key_span].astype(jnp.float32)
        allowed = (seg_query[:, :, None] == seg_keys[:, None, :]) & (
            query_place[None, :, None] >= key_place[None, None, :]
        )
        return (key_block, value_block, allowed)

    def block_scores(key_block, allowed):
        raw_scores = (
            jnp.einsum("sckgd,sbkd->skgcb", queries, key_block, preferred_element_type=jnp.float32)
            * score_scale
        )
        return jnp.where(allowed[:, None, None, :, :], raw_scores, masked_score)

    row_peak = jnp.full((seq_count, KV, groups, local_rows), masked_score, jnp.float32)
    exp_total = jnp.zeros((seq_count, KV, groups, local_rows), jnp.float32)
    for block_index in range(block_count):
        key_block, value_block, allowed = block_parts(block_index)

        def first_pass(carried, key_block=key_block, allowed=allowed):
            peak_old, total_old = carried
            masked = block_scores(key_block, allowed)
            peak_new = jnp.maximum(peak_old, jnp.max(masked, axis=-1))
            total_new = total_old * jnp.exp(peak_old - peak_new) + jnp.sum(
                jnp.exp(masked - peak_new[..., None]), axis=-1
            )
            return ((peak_new, total_new), nothing)

        (row_peak, exp_total), unused = first_pass((row_peak, exp_total))
    log_total = row_peak + jnp.log(exp_total)
    mixed_heads = jnp.zeros((seq_count, local_rows, KV, groups, HD), jnp.float32)
    for block_index in range(block_count):
        key_block, value_block, allowed = block_parts(block_index)

        def second_pass(carried, key_block=key_block, value_block=value_block, allowed=allowed):
            masked = block_scores(key_block, allowed)
            soft_prob = jnp.exp(masked - log_total[..., None]).astype(jnp.bfloat16)
            added = jnp.einsum(
                "skgcb,sbkd->sckgd", soft_prob, value_block, preferred_element_type=jnp.float32
            )
            return (carried + added, nothing)

        mixed_heads, unused = second_pass(mixed_heads)
    mixed_low = mixed_heads.reshape(seq_count, local_rows, D).astype(jnp.bfloat16)
    branch = jnp.einsum("sci,io->sco", mixed_low, w_out, preferred_element_type=jnp.float32)
    residual = x_wide + branch
    inv_two = lax.rsqrt(jnp.mean(residual * residual, axis=-1, keepdims=True) + norm_eps)
    normed_two = (residual * inv_two * gain_two).astype(jnp.bfloat16)
    gate_up = jnp.einsum("scd,df->scf", normed_two, w_gu, preferred_element_type=jnp.float32)
    gate_part = gate_up[..., :FF]
    up_part = gate_up[..., FF:]
    sigmoid_gate = jax.nn.sigmoid(gate_part)
    silu_gate = gate_part * sigmoid_gate
    hidden = (silu_gate * up_part).astype(jnp.bfloat16)
    result = (
        residual + jnp.einsum("scf,fd->scd", hidden, w_down, preferred_element_type=jnp.float32)
    ).astype(jnp.bfloat16)
    grad_down = jnp.einsum("scf,scd->fd", hidden, cotangent, preferred_element_type=jnp.float32)
    grad_hidden = jnp.einsum("scd,fd->scf", cotangent, w_down, preferred_element_type=jnp.float32)
    grad_gate = grad_hidden * up_part * sigmoid_gate * (1.0 + gate_part * (1.0 - sigmoid_gate))
    grad_up = grad_hidden * silu_gate
    grad_gu = jnp.concatenate([grad_gate, grad_up], axis=-1).astype(jnp.bfloat16)
    grad_w_gu = jnp.einsum("scd,scf->df", normed_two, grad_gu, preferred_element_type=jnp.float32)
    grad_normed_two = jnp.einsum("scf,df->scd", grad_gu, w_gu, preferred_element_type=jnp.float32)
    grad_in_two, grad_gain_two = norm_back(residual, inv_two, gain_two, grad_normed_two)
    grad_residual = cotangent.astype(jnp.float32) + grad_in_two
    ffn_local = jnp.concatenate([grad_w_gu.reshape(-1), grad_down.reshape(-1)]) * token_scale
    grad_branch = grad_residual.astype(jnp.bfloat16)
    grad_w_out = jnp.einsum(
        "sci,sco->io", mixed_low, grad_branch, preferred_element_type=jnp.float32
    )
    grad_mixed = jnp.einsum("sco,io->sci", grad_branch, w_out, preferred_element_type=jnp.float32)
    grad_mixed = grad_mixed.astype(jnp.bfloat16).reshape(seq_count, local_rows, KV, groups, HD)
    row_delta = jnp.zeros((seq_count, KV, groups, local_rows), jnp.float32)
    for block_index in range(block_count):
        key_block, value_block, allowed = block_parts(block_index)

        def delta_pass(carried, key_block=key_block, value_block=value_block, allowed=allowed):
            masked = block_scores(key_block, allowed)
            soft_prob = jnp.exp(masked - log_total[..., None])
            grad_prob = jnp.einsum(
                "sckgd,sbkd->skgcb", grad_mixed, value_block, preferred_element_type=jnp.float32
            )
            return (carried + jnp.sum(soft_prob * grad_prob, axis=-1), nothing)

        row_delta, unused = delta_pass(row_delta)
    grad_queries = jnp.zeros((seq_count, local_rows, KV, groups, HD), jnp.float32)
    key_pieces = []
    value_pieces = []
    for block_index in range(block_count):
        key_block, value_block, allowed = block_parts(block_index)

        def grad_pass(carried, key_block=key_block, value_block=value_block, allowed=allowed):
            masked = block_scores(key_block, allowed)
            soft_prob = jnp.exp(masked - log_total[..., None])
            prob_low = soft_prob.astype(jnp.bfloat16)
            grad_prob = jnp.einsum(
                "sckgd,sbkd->skgcb", grad_mixed, value_block, preferred_element_type=jnp.float32
            )
            grad_score = (soft_prob * (grad_prob - row_delta[..., None])).astype(jnp.bfloat16)
            query_add = (
                jnp.einsum(
                    "skgcb,sbkd->sckgd", grad_score, key_block, preferred_element_type=jnp.float32
                )
                * score_scale
            )
            grad_key = (
                jnp.einsum(
                    "skgcb,sckgd->sbkd", grad_score, queries, preferred_element_type=jnp.float32
                )
                * score_scale
            )
            grad_value = jnp.einsum(
                "skgcb,sckgd->sbkd", prob_low, grad_mixed, preferred_element_type=jnp.float32
            )
            return (
                carried + query_add,
                (
                    grad_key.reshape(seq_count, key_span, kv_width),
                    grad_value.reshape(seq_count, key_span, kv_width),
                ),
            )

        grad_queries, block_grads = grad_pass(grad_queries)
        key_pieces.append(block_grads[0])
        value_pieces.append(block_grads[1])
    key_grad_all = jnp.concatenate(key_pieces, axis=1)
    value_grad_all = jnp.concatenate(value_pieces, axis=1)
    key_grad, value_grad = (
        lax.psum_scatter(
            key_grad_all.astype(jnp.bfloat16), "seq", scatter_dimension=1, tiled=True
        ).astype(jnp.float32),
        lax.psum_scatter(
            value_grad_all.astype(jnp.bfloat16), "seq", scatter_dimension=1, tiled=True
        ).astype(jnp.float32),
    )
    query_pre = rotate_back(grad_queries, cos_query, sin_query).reshape(seq_count, local_rows, D)
    key_pre = rotate_back(
        key_grad.reshape(seq_count, local_rows, KV, HD), cos_key, sin_key
    ).reshape(seq_count, local_rows, kv_width)
    grad_qkv = jnp.concatenate([query_pre, key_pre, value_grad], axis=-1).astype(jnp.bfloat16)
    grad_bias = jnp.sum(grad_qkv.astype(jnp.float32), axis=(0, 1))
    grad_w_qkv = jnp.einsum("scd,sce->de", normed_one, grad_qkv, preferred_element_type=jnp.float32)
    grad_normed_one = jnp.einsum("sce,de->scd", grad_qkv, w_qkv, preferred_element_type=jnp.float32)
    grad_in_one, grad_gain_one = norm_back(x_wide, inv_one, gain_one, grad_normed_one)
    grad_input = grad_residual + grad_in_one
    used_entries = 3 * D + 2 * kv_width + D * (2 * D + 2 * kv_width)
    padding = attn_master.shape[0] * seq_parts - used_entries
    attn_local = (
        jnp.concatenate(
            [
                grad_gain_one,
                grad_gain_two,
                grad_bias,
                grad_w_qkv.reshape(-1),
                grad_w_out.reshape(-1),
                jnp.zeros((padding,), jnp.float32),
            ]
        )
        * token_scale
    )
    attn_owned, ffn_owned = (
        lax.psum_scatter(
            attn_local.astype(jnp.bfloat16), "seq", scatter_dimension=0, tiled=True
        ).astype(jnp.float32),
        lax.psum_scatter(
            ffn_local.astype(jnp.bfloat16), "seq", scatter_dimension=0, tiled=True
        ).astype(jnp.float32),
    )
    grad_attn, grad_ffn = (
        lax.psum(attn_owned.astype(jnp.bfloat16), "dp").astype(jnp.float32),
        lax.psum(ffn_owned.astype(jnp.bfloat16), "dp").astype(jnp.float32),
    )
    attn_change, moment_attn, second_attn = adam_step(
        attn_master, attn_moment, attn_second, grad_attn
    )
    ffn_change, moment_ffn, second_ffn = adam_step(ffn_master, ffn_moment, ffn_second, grad_ffn)
    return (
        result,
        grad_input,
        attn_change,
        moment_attn,
        second_attn,
        grad_attn,
        ffn_change,
        moment_ffn,
        second_ffn,
        grad_ffn,
    )


def solution(mesh):
    in_specs = (
        P("dp", "seq", None),
        P("dp", "seq", None),
        P("dp", "seq"),
        P("dp", "seq"),
        P("seq"),
        P("seq"),
        P("seq"),
        P("seq"),
        P("seq"),
        P("seq"),
    )
    out_specs = (
        P("dp", "seq", None),
        P("dp", "seq", None),
        P("seq"),
        P("seq"),
        P("seq"),
        P("seq"),
        P("seq"),
        P("seq"),
        P("seq"),
        P("seq"),
    )
    return jax.shard_map(
        per_device, mesh=mesh, in_specs=in_specs, out_specs=out_specs, check_vma=False
    )
```

profile of v0, /device:TPU:0, one launch (start us, length us, event | category | flops | bytes accessed | tf_op | source)
XLA Modules:
  0.0 1687.3 jit_solution(13379455358743474625)
XLA Ops:
  17.3 50.1 %all-gather.12.cloned.1.call-done = bf16[8,1,229760]{2,1,0:T(2,128)(2,1)} async-done(((bf16[1,1,229760]{2,1,0:T(2,128)(2,1)}), bf16[8,1,229760]{2,1,0:T(2,128)(2,1)}) %all-gather.12.cloned.1.call-update) | async-done | bytes 3676176 | tf_op jit(solution)/shard_map/all_gather | solution.py:110
  67.4 79.1 %reduce = bf16[8,229760]{1,0:T(8,128)(2,1)} reduce(bf16[8,1,229760]{2,1,0:T(2,128)(2,1)} %all-gather.12.cloned.1.call-done, bf16[]{:T(256)} %constant.76), dimensions={1}, to_apply=%all-gather.reduce_sub_computation | reduce | bytes 7352322 | tf_op jit(solution)/shard_map/all_gather | solution.py:110
  146.5 9.3 reshape.455
  179.0 8.9 all_gather.17
  218.9 10.9 all-gather.8.cloned.1.call-done
  232.4 15.9 fusion.20
  248.4 11.8 fusion.21
  260.2 11.8 fusion.19
  272.0 15.8 fusion.18
  287.9 17.6 %exponential_reduce_fusion = f32[4,2,7,256]{3,2,1,0:T(8,128)S(1)} fusion(f32[4,2,512,256,7]{3,2,4,1,0:T(8,128)} %get-tuple-element.80, f32[4,2,7,256]{3,2,1,0:T(8,128)S(1)} %get-tuple-element.30, pred[4,256,512]{1,2,0:T(8,128)(4,1)S(1)} %get-tuple-element.72), kind=kLoop, calls=%fused_computation.30 | loop fusion | flops 29345792 | bytes 29999104 | tf_op jit(solution)/shard_map/reduce_sum | solution.py:175
  312.4 13.2 exponential_reduce_fusion.2
  325.6 13.2 exponential_reduce_fusion.3
  339.0 15.2 fusion.54
  354.2 15.3 fusion.60
  369.5 14.8 fusion.57
  384.3 17.9 %add_convert_fusion.1 = bf16[4,2,64,7,256]{4,2,3,1,0:T(8,128)(2,1)} fusion(f32[4,2,64,7,256]{4,2,3,1,0:T(8,128)} %fusion.54, f32[4,2,64,7,256]{4,2,3,1,0:T(8,128)} %fusion.60, f32[4,2,64,7,256]{4,2,3,1,0:T(8,128)} %fusion.57, bf16[4,512,2,64,1]{1,3,4,2,0:T(8,128)(2,1)S(1)} %bitcast.284, f32[4,2,512,256,7]{3,2,4,1,0:T(8,128)} %get-tuple-element.80, ...), kind=kOutput, calls=%fused_computation.81 | convolution fusion | flops 972554240 | bytes 43311104 | tf_op jit(solution)/shard_map/skgcb,sbkd->sckgd/dot_general | solution.py:189
  409.1 12.5 slice.207
  421.7 29.8 %reshape.466 = bf16[896,9728,1]{1,0,2:T(8,128)(2,1)} reshape(bf16[8716288]{0:T(1024)(128)(2,1)} %slice.207) | data formatting | bytes 34865152 | tf_op jit(solution)/shard_map/slice | solution.py:32
  460.1 16.4 reshape.467
  476.6 30.4 %fusion.50 = f32[4,256,9728]{2,1,0:T(8,128)} fusion(bf16[896,9728,1]{1,0,2:T(8,128)(2,1)} %reshape.466, f32[4,256,896]{2,1,0:T(8,128)} %get-tuple-element.88, f32[896]{0:T(1024)S(1)} %copy-done.60, f32[4,256]{1,0:T(4,128)S(1)} %get-tuple-element.68), kind=kOutput, calls=%fused_computation.125 | convolution fusion | flops 17853710336 | bytes 60956160 | tf_op jit(solution)/shard_map/scd,df->scf/dot_general | solution.py:200
  507.0 30.5 %multiply_convert_fusion.1 = (bf16[4,256,4864]{2,1,0:T(8,128)(2,1)}, bf16[4,256,4864]{2,1,0:T(8,128)(2,1)}, bf16[4,256,4864]{2,1,0:T(8,128)(2,1)}) fusion(f32[4,256,9728]{2,1,0:T(8,128)} %fusion.50, bf16[4,256,896]{2,1,0:T(8,128)(2,1)S(1)} %copy-done.48, bf16[4864,896,1]{1,0,2:T(8,128)(2,1)} %reshape.467), kind=kOutput, calls=%fused_computation.41 | convolution fusion | flops 9000189952 | bytes 80281600 | tf_op jit(solution)/shard_map/scd,fd->scf/dot_general | solution.py:210
  537.5 30.4 %multiply_reduce_fusion = (f32[896]{0:T(1024)}, f32[4,256]{1,0:T(4,128)S(1)}, f32[4,256,896]{2,1,0:T(8,128)}) fusion(f32[4,256,896]{2,1,0:T(8,128)} %get-tuple-element.88, f32[4,256]{1,0:T(4,128)S(1)} %get-tuple-element.68, f32[896]{0:T(1024)S(1)} %copy-done.60, bf16[896,9728,1]{1,0,2:T(8,128)(2,1)} %reshape.466, ...), kind=kOutput, calls=%fused_computation.74 | convolution fusion | flops 17896308736 | bytes 44710912 | tf_op jit(solution)/shard_map/scf,df->scd/dot_general | solution.py:215
  579.3 13.8 fusion.46
  593.1 13.6 fusion.45
  606.7 13.6 fusion.44
  620.4 13.9 fusion.43
  634.3 11.6 fusion.93
  645.9 11.6 fusion.94
  657.5 11.7 fusion.95
  669.2 27.2 %convolution_bitcast_fusion = f32[896,9728]{1,0:T(8,128)} fusion(bf16[4,256,4864]{2,1,0:T(8,128)(2,1)} %get-tuple-element.34, bf16[4,256,4864]{2,1,0:T(8,128)(2,1)} %get-tuple-element.33, f32[4,256,896]{2,1,0:T(8,128)S(1)} %copy-done.32, f32[896]{0:T(1024)S(1)} %copy-done.60, f32[4,256]{1,0:T(4,128)S(1)} %get-tuple-element.68), kind=kOutput, calls=%fused_computation.38 | convolution fusion | flops 17893556224 | bytes 58465792 | tf_op jit(solution)/shard_map/scd,scf->df/dot_general | solution.py:214
  704.6 75.6 %fusion.7 = (f32[4,2,7,256]{3,2,1,0:T(8,128)}, f32[4,2,7,256]{3,2,1,0:T(8,128)}, f32[4,2,7,256]{3,2,1,0:T(8,128)}, f32[4,2,7,256]{3,2,1,0:T(8,128)}, f32[4,2,512,256,7]{3,2,4,1,0:T(8,128)}) fusion(f32[4,2,512,256,7]{3,2,4,1,0:T(8,128)} %get-tuple-element.84, f32[4,2,7,256]{3,2,1,0:T(8,128)S(1)} %copy-done.51, pred[4,256,512]{1,2,0:T(8,128)(4,1)S(1)} %copy-done.10, ...), kind=kOutput, calls=%fused_computation.14 | convolution fusion | flops 1086267392 | bytes 239624192 | tf_op jit(solution)/shard_map/sckgd,sbkd->skgcb/dot_general | solution.py:232
  781.1 92.1 %fusion.12 = (bf16[4,2,7,256,512]{3,4,2,1,0:T(8,128)(2,1)}, bf16[4,2,7,256,512]{3,4,2,1,0:T(8,128)(2,1)}, bf16[4,2,7,256,512]{3,4,2,1,0:T(8,128)(2,1)}, bf16[4,2,7,256,512]{3,4,2,1,0:T(8,128)(2,1)}) fusion(f32[4,2,512,256,7]{3,2,4,1,0:T(8,128)} %fusion.93, f32[4,2,512,256,7]{3,2,4,1,0:T(8,128)} %get-tuple-element.86, f32[4,2,7,256]{3,2,1,0:T(8,128)S(1)} %add_add_fusion, ...), kind=kLoop, calls=%fused_computation.21 | loop fusion | flops 176160768 | bytes 295813120 | tf_op jit(solution)/shard_map/convert_element_type | solution.py:251
  873.2 9.7 fusion.42
  882.9 9.7 fusion.41
  892.6 9.7 fusion.40
  902.3 10.5 fusion.39
  915.5 17.5 %convolution_bitcast_fusion.1 = f32[4864,896]{1,0:T(8,128)} fusion(bf16[4,256,4864]{2,1,0:T(8,128)(2,1)} %get-tuple-element.35, bf16[4,256,896]{2,1,0:T(8,128)(2,1)} %param.11), kind=kOutput, calls=%fused_computation.50 | convolution fusion | flops 8925478912 | bytes 29229056 | tf_op jit(solution)/shard_map/scf,scd->fd/dot_general | solution.py:209
  933.0 18.6 %reshape.451 = f32[4358144]{0:T(1024)} reshape(f32[4864,896]{1,0:T(8,128)} %convolution_bitcast_fusion.1) | data formatting | bytes 34865152 | tf_op jit(solution)/shard_map/reshape | solution.py:218
  951.6 33.4 %reshape.450 = f32[8716288]{0:T(1024)} reshape(f32[896,9728]{1,0:T(8,128)} %convolution_bitcast_fusion) | data formatting | bytes 69730304 | tf_op jit(solution)/shard_map/reshape | solution.py:218
  986.5 9.7 fusion.98
  996.2 9.6 fusion.96
  1005.9 27.8 %fusion = bf16[13074432]{0:T(1024)(128)(2,1)} fusion(f32[4358144]{0:T(1024)} %reshape.451, f32[8716288]{0:T(1024)} %reshape.450), kind=kLoop, calls=%fused_computation.1 | loop fusion | flops 39223296 | bytes 78446592 | tf_op jit(solution)/shard_map/convert_element_type | solution.py:318
  1089.2 36.1 %dynamic-update-slice.3 = f32[1838080]{0:T(1024)} dynamic-update-slice(f32[1838080]{0:T(1024)} %constant_dynamic-update-slice_fusion.1, f32[1032192]{0:T(1024)} %reshape.448, s32[]{} %constant.81) | dynamic-update-slice | bytes 8257540
  1125.2 26.8 %dynamic-update-slice.4 = f32[1838080]{0:T(1024)} dynamic-update-slice(f32[1838080]{0:T(1024)} %dynamic-update-slice.3, f32[802816]{0:T(1024)S(1)} %reshape.449, s32[]{} %constant.82) | dynamic-update-slice | bytes 6422532
  1160.5 356.4 %all-reduce.7.cloned.1.call-done = (bf16[1838080]{0:T(1024)(128)(2,1)}, bf16[13074432]{0:T(1024)(128)(2,1)}) async-done(((bf16[1838080]{0:T(1024)(128)(2,1)}, bf16[13074432]{0:T(1024)(128)(2,1)}), (bf16[1838080]{0:T(1024)(128)(2,1)}, bf16[13074432]{0:T(1024)(128)(2,1)})) %all-reduce.7.cloned.1.call-update) | async-done | bytes 29825040
  1522.2 17.4 %add_convert_fusion = bf16[4,256,896]{2,1,0:T(8,128)(2,1)} fusion(f32[4,256,896]{2,1,0:T(8,128)} %get-tuple-element.88, bf16[4,256,4864]{2,1,0:T(8,128)(2,1)} %get-tuple-element.35, bf16[4864,896,1]{1,0,2:T(8,128)(2,1)} %reshape.467), kind=kOutput, calls=%fused_computation.78 | convolution fusion | flops 8927313920 | bytes 24182784 | tf_op jit(solution)/shard_map/scf,fd->scd/dot_general | solution.py:207
  1542.0 120.7 %all-reduce.9.cloned.1.call-done = (bf16[229760]{0:T(1024)(128)(2,1)}, bf16[1634304]{0:T(1024)(128)(2,1)}) async-done(((bf16[229760]{0:T(1024)(128)(2,1)}, bf16[1634304]{0:T(1024)(128)(2,1)}), (bf16[229760]{0:T(1024)(128)(2,1)}, bf16[1634304]{0:T(1024)(128)(2,1)})) %all-reduce.9.cloned.1.call-update) | async-done | bytes 3728144 | tf_op jit(solution)/shard_map/psum | solution.py:322
  1665.9 14.3 add_multiply_fusion
  (247 shorter events, 187.3 us)
Async XLA Ops:
  7.2 60.2 %all-gather.12.cloned.1.call-start = ((), (), s32[]{:S(2)}) async-start(), calls=%async_computation.7 | async-start | bytes 8271360 | tf_op jit(solution)/shard_map/all_gather | solution.py:110
  14.5 192.7 %all-gather.6.cloned.1.call-start = ((), (), s32[]{:S(2)}) async-start(), calls=%async_computation.2 | async-start | bytes 2359296 | tf_op jit(solution)/shard_map/all_gather | solution.py:135
  17.3 146.4 %copy-start.56 = (f32[4,256]{1,0:T(4,128)}, f32[4,256]{1,0:T(4,128)S(1)}, u32[]{:S(2)}) copy-start(f32[4,256]{1,0:T(4,128)S(1)} %get-tuple-element.66) | copy-start | bytes 12292
  171.7 58.2 %all-gather.8.cloned.1.call-start = ((), (), s32[]{:S(2)}) async-start(), calls=%async_computation.3 | async-start | bytes 2359296 | tf_op jit(solution)/shard_map/all_gather | solution.py:134
  172.3 32.1 %copy-start.34 = (f32[4,256,32]{1,2,0:T(8,128)}, f32[4,256,32]{1,2,0:T(8,128)S(1)}, u32[]{:S(2)}) copy-start(f32[4,256,32]{1,2,0:T(8,128)S(1)} %get-tuple-element.63) | copy-start | bytes 393220
  172.3 32.1 %copy-start.36 = (f32[4,256,32]{1,2,0:T(8,128)}, f32[4,256,32]{1,2,0:T(8,128)S(1)}, u32[]{:S(2)}) copy-start(f32[4,256,32]{1,2,0:T(8,128)S(1)} %get-tuple-element.64) | copy-start | bytes 393220
  174.6 234.5 %all-gather.10.cloned.1.call-start = ((), (), s32[]{:S(2)}) async-start(), calls=%async_computation.4 | async-start | bytes 29417472 | tf_op jit(solution)/shard_map/all_gather | solution.py:111
  178.9 883.4 %reduce-scatter.3.cloned.1.call-start = ((), (), s32[]{:S(2)}) async-start(), calls=%async_computation.5 | async-start | bytes 2359296 | tf_op jit(solution)/shard_map/reduce_scatter | solution.py:281
  191.0 69.2 %copy-start.8 = (pred[4,256,512]{1,2,0:T(8,128)(4,1)}, pred[4,256,512]{1,2,0:T(8,128)(4,1)S(1)}, u32[]{:S(2)}) copy-start(pred[4,256,512]{1,2,0:T(8,128)(4,1)S(1)} %get-tuple-element.70) | copy-start | bytes 1572868
  191.0 193.3 %copy-start.4 = (pred[4,256,512]{1,2,0:T(8,128)(4,1)}, pred[4,256,512]{1,2,0:T(8,128)(4,1)S(1)}, u32[]{:S(2)}) copy-start(pred[4,256,512]{1,2,0:T(8,128)(4,1)S(1)} %get-tuple-element.72) | copy-start | bytes 1572868
  207.1 64.8 %copy-start = (bf16[4,256,2,7,32]{1,4,3,2,0:T(8,128)(2,1)}, bf16[4,256,2,7,32]{1,4,3,2,0:T(8,128)(2,1)S(1)}, u32[]{:S(2)}) copy-start(bf16[4,256,2,7,32]{1,4,3,2,0:T(8,128)(2,1)S(1)} %get-tuple-element.38) | copy-start | bytes 2752516
  207.2 64.8 %copy-start.2 = (bf16[4,256,2,7,32]{1,4,3,2,0:T(8,128)(2,1)}, bf16[4,256,2,7,32]{1,4,3,2,0:T(8,128)(2,1)S(1)}, u32[]{:S(2)}) copy-start(bf16[4,256,2,7,32]{1,4,3,2,0:T(8,128)(2,1)S(1)} %get-tuple-element.39) | copy-start | bytes 2752516
  232.4 15.9 copy-start.27
  232.4 15.9 copy-start.22
  232.4 27.8 %copy-start.24 = (bf16[4,512,128]{1,2,0:T(8,128)(2,1)}, bf16[4,512,128]{1,2,0:T(8,128)(2,1)S(1)}, u32[]{:S(2)}) copy-start(bf16[4,512,128]{1,2,0:T(8,128)(2,1)S(1)} %get-tuple-element.49) | copy-start | bytes 1572868
  272.0 33.5 %slice-start = ((s8[29360128]{0:T(1024)(128)(4,1)}), s8[4194304]{0:T(1024)(128)(4,1)S(1)}, s32[]{:S(2)}) async-start(s8[29360128]{0:T(1024)(128)(4,1)} %bitcast.272), calls=%async_computation.10 | async-start | bytes 8388608
  272.0 33.5 %slice-start.1 = ((s8[29360128]{0:T(1024)(128)(4,1)}), s8[4194304]{0:T(1024)(128)(4,1)S(1)}, s32[]{:S(2)}) async-start(s8[29360128]{0:T(1024)(128)(4,1)} %bitcast.272), calls=%async_computation.11 | async-start | bytes 8388608
  272.0 33.5 %slice-start.2 = ((s8[29360128]{0:T(1024)(128)(4,1)}), s8[4194304]{0:T(1024)(128)(4,1)S(1)}, s32[]{:S(2)}) async-start(s8[29360128]{0:T(1024)(128)(4,1)} %bitcast.272), calls=%async_computation.12 | async-start | bytes 8388608
  272.0 33.5 %slice-start.3 = ((s8[29360128]{0:T(1024)(128)(4,1)}), s8[4194304]{0:T(1024)(128)(4,1)S(1)}, s32[]{:S(2)}) async-start(s8[29360128]{0:T(1024)(128)(4,1)} %bitcast.272), calls=%async_computation.13 | async-start | bytes 8388608
  287.8 17.7 %slice-start.4 = ((s8[29360128]{0:T(1024)(128)(4,1)}), s8[4194304]{0:T(1024)(128)(4,1)S(1)}, s32[]{:S(2)}) async-start(s8[29360128]{0:T(1024)(128)(4,1)} %bitcast.272), calls=%async_computation.14 | async-start | bytes 8388608
  287.8 17.7 %slice-start.5 = ((s8[29360128]{0:T(1024)(128)(4,1)}), s8[4194304]{0:T(1024)(128)(4,1)S(1)}, s32[]{:S(2)}) async-start(s8[29360128]{0:T(1024)(128)(4,1)} %bitcast.272), calls=%async_computation.15 | async-start | bytes 8388608
  287.9 17.7 %slice-start.6 = ((s8[29360128]{0:T(1024)(128)(4,1)}), s8[4194304]{0:T(1024)(128)(4,1)S(1)}, s32[]{:S(2)}) async-start(s8[29360128]{0:T(1024)(128)(4,1)} %bitcast.272), calls=%async_computation.16 | async-start | bytes 8388608
  287.9 17.7 %copy-start.11 = (pred[4,256,512]{1,2,0:T(8,128)(4,1)S(1)}, pred[4,256,512]{1,2,0:T(8,128)(4,1)}, u32[]{:S(2)}) copy-start(pred[4,256,512]{1,2,0:T(8,128)(4,1)} %get-tuple-element.71) | copy-start | bytes 1572868
  338.9 45.4 %copy-start.50 = (f32[4,2,7,256]{3,2,1,0:T(8,128)}, f32[4,2,7,256]{3,2,1,0:T(8,128)S(1)}, u32[]{:S(2)}) copy-start(f32[4,2,7,256]{3,2,1,0:T(8,128)S(1)} %log_add_fusion) | copy-start | bytes 172036
  354.2 15.3 copy-start.39
  384.3 17.9 %copy-start.17 = (bf16[4,256,896]{2,1,0:T(8,128)(2,1)S(1)}, bf16[4,256,896]{2,1,0:T(8,128)(2,1)}, u32[]{:S(2)}) copy-start(bf16[4,256,896]{2,1,0:T(8,128)(2,1)} %param.10) | copy-start | bytes 5505028
  460.1 16.4 copy-start.60
  476.5 30.4 %copy-start.48 = (bf16[4,256,896]{2,1,0:T(8,128)(2,1)S(1)}, bf16[4,256,896]{2,1,0:T(8,128)(2,1)}, u32[]{:S(2)}) copy-start(bf16[4,256,896]{2,1,0:T(8,128)(2,1)} %param.11) | copy-start | bytes 5505028
  537.5 30.4 %copy-start.31 = (f32[4,256,896]{2,1,0:T(8,128)S(1)}, f32[4,256,896]{2,1,0:T(8,128)}, u32[]{:S(2)}) copy-start(f32[4,256,896]{2,1,0:T(8,128)} %get-tuple-element.88) | copy-start | bytes 11010052
  537.5 30.4 %copy-start.61 = (f32[4,256]{1,0:T(4,128)S(1)}, f32[4,256]{1,0:T(4,128)}, u32[]{:S(2)}) copy-start(f32[4,256]{1,0:T(4,128)} %get-tuple-element.67) | copy-start | bytes 12292
  781.1 92.1 %copy-start.1 = (bf16[4,256,2,7,32]{1,4,3,2,0:T(8,128)(2,1)S(1)}, bf16[4,256,2,7,32]{1,4,3,2,0:T(8,128)(2,1)}, u32[]{:S(2)}) copy-start(bf16[4,256,2,7,32]{1,4,3,2,0:T(8,128)(2,1)} %copy-done) | copy-start | bytes 2752516
  781.1 92.1 %copy-start.3 = (bf16[4,256,2,7,32]{1,4,3,2,0:T(8,128)(2,1)S(1)}, bf16[4,256,2,7,32]{1,4,3,2,0:T(8,128)(2,1)}, u32[]{:S(2)}) copy-start(bf16[4,256,2,7,32]{1,4,3,2,0:T(8,128)(2,1)} %copy-done.2) | copy-start | bytes 2752516
  915.5 149.8 %reduce-scatter.5.cloned.1.call-start = ((), (), s32[]{:S(2)}) async-start(), calls=%async_computation.6 | async-start | bytes 2359296 | tf_op jit(solution)/shard_map/reduce_scatter | solution.py:284
  951.6 33.4 %copy-start.44 = (bf16[4,512,128]{2,1,0:T(8,128)(2,1)S(1)}, bf16[4,512,128]{2,1,0:T(8,128)(2,1)}, u32[]{:S(2)}) copy-start(bf16[4,512,128]{2,1,0:T(8,128)(2,1)} %copy.127) | copy-start | bytes 1572868
  951.6 33.4 %copy-start.45 = (bf16[4,512,128]{2,1,0:T(8,128)(2,1)S(1)}, bf16[4,512,128]{2,1,0:T(8,128)(2,1)}, u32[]{:S(2)}) copy-start(bf16[4,512,128]{2,1,0:T(8,128)(2,1)} %copy.126) | copy-start | bytes 1572868
  951.6 33.4 %copy-start.46 = (bf16[4,512,128]{2,1,0:T(8,128)(2,1)S(1)}, bf16[4,512,128]{2,1,0:T(8,128)(2,1)}, u32[]{:S(2)}) copy-start(bf16[4,512,128]{2,1,0:T(8,128)(2,1)} %copy.125) | copy-start | bytes 1572868
  951.6 33.4 %copy-start.47 = (bf16[4,512,128]{2,1,0:T(8,128)(2,1)S(1)}, bf16[4,512,128]{2,1,0:T(8,128)(2,1)}, u32[]{:S(2)}) copy-start(bf16[4,512,128]{2,1,0:T(8,128)(2,1)} %copy.124) | copy-start | bytes 1572868
  951.6 34.9 %copy-start.28 = (bf16[4,512,128]{1,2,0:T(8,128)(2,1)S(1)}, bf16[4,512,128]{1,2,0:T(8,128)(2,1)}, u32[]{:S(2)}) copy-start(bf16[4,512,128]{1,2,0:T(8,128)(2,1)} %copy-done.27) | copy-start | bytes 1572868
  1005.9 27.9 %copy-start.25 = (bf16[4,512,128]{1,2,0:T(8,128)(2,1)S(1)}, bf16[4,512,128]{1,2,0:T(8,128)(2,1)}, u32[]{:S(2)}) copy-start(bf16[4,512,128]{1,2,0:T(8,128)(2,1)} %copy-done.24) | copy-start | bytes 1572868
  1005.9 511.0 %all-reduce.7.cloned.1.call-start = ((), (), s32[]{:S(2)}) async-start(), calls=%async_computation.8 | async-start | bytes 59650048
  1158.0 504.7 %all-reduce.9.cloned.1.call-start = ((), (), s32[]{:S(2)}) async-start(), calls=%async_computation.9 | async-start | bytes 7458816 | tf_op jit(solution)/shard_map/psum | solution.py:322
  1522.2 17.4 %copy-start.16 = (f32[4,256,896]{2,1,0:T(8,128)S(1)}, f32[4,256,896]{2,1,0:T(8,128)}, u32[]{:S(2)}) copy-start(f32[4,256,896]{2,1,0:T(8,128)} %copy-done.15) | copy-start | bytes 11010052
  1522.2 17.4 %copy-start.18 = (bf16[4,256,896]{2,1,0:T(8,128)(2,1)S(1)}, bf16[4,256,896]{2,1,0:T(8,128)(2,1)}, u32[]{:S(2)}) copy-start(bf16[4,256,896]{2,1,0:T(8,128)(2,1)} %param.10) | copy-start | bytes 5505028
  1522.2 17.4 %copy-start.33 = (f32[4,256,896]{2,1,0:T(8,128)S(1)}, f32[4,256,896]{2,1,0:T(8,128)}, u32[]{:S(2)}) copy-start(f32[4,256,896]{2,1,0:T(8,128)} %get-tuple-element.91) | copy-start | bytes 11010052
  1522.2 17.4 %copy-start.55 = (f32[4,256]{1,0:T(4,128)S(1)}, f32[4,256]{1,0:T(4,128)}, u32[]{:S(2)}) copy-start(f32[4,256]{1,0:T(4,128)} %get-tuple-element.65) | copy-start | bytes 12292
  1539.6 123.1 %copy-start.30 = (f32[229760]{0:T(1024)S(1)}, f32[229760]{0:T(1024)}, u32[]{:S(2)}) copy-start(f32[229760]{0:T(1024)} %param.14) | copy-start | bytes 2757124
  1539.6 123.1 %copy-start.52 = (f32[229760]{0:T(1024)S(1)}, f32[229760]{0:T(1024)}, u32[]{:S(2)}) copy-start(f32[229760]{0:T(1024)} %param.15) | copy-start | bytes 2757124
  1539.6 123.1 %copy-start.53 = (f32[229760]{0:T(1024)S(1)}, f32[229760]{0:T(1024)}, u32[]{:S(2)}) copy-start(f32[229760]{0:T(1024)} %param.16) | copy-start | bytes 2757124
  (33 other events, 291.6 us)
Sparse Core Ops, SparseCore 0:
  14.6 52.6 all-gather.11
  171.8 27.9 all-gather.5
  201.7 28.1 all-gather.7
  232.2 129.4 all-gather.9
  915.6 41.1 reduce-scatter.2
  1006.0 41.2 reduce-scatter.4
  1158.1 358.7 all-reduce.6
  1522.3 140.3 all-reduce.8
where the time goes:
time: 1700 us; the launch traced here: 1690 us
  matrix products  548 us (32%)
  waiting for transfers between devices  538 us (32%)
  other arithmetic  304 us (18%)
  local copies, waits for them, and re-layouts  271 us (16%)
    unnamed x9, waiting for transfers between devices  356 us
    psum x1, waiting for transfers between devices, per_device(): lax.psum(attn_owned.astype(jnp.bfloat16), 'dp').astype(jnp.float32)  121 us
    dot_general x3, matrix products, delta_pass(): jnp.einsum('sckgd,sbkd->skgcb', grad_mixed, value_block, preferred_elemen...  98.9 us
    unnamed x156, local copies, waits for them, and re-layouts  92.9 us
    convert_element_type x1, other arithmetic, grad_pass(): (soft_prob * (grad_prob - row_delta[..., None])).astype(jnp.bfloat16)  92.1 us
    all_gather x1, other arithmetic, per_device(): lax.all_gather(attn_master.astype(jnp.bfloat16), 'seq', axis=0, tiled=True)  79.1 us
    dot_general x4, matrix products, second_pass(): jnp.einsum('skgcb,sbkd->sckgd', soft_prob, value_block, preferred_element...  63.2 us
    dot_general x4, matrix products, block_scores(): jnp.einsum('sckgd,sbkd->skgcb', queries, key_block, preferred_element_typ...  55.3 us
  transfers between devices with their start and end apart: 8, of which 4 were waited for; matrix products, arithmetic and copies ran while one was open for 23% of the time, Pallas kernels for 0%

commit v1 on v0

--- a/solution.py
+++ b/solution.py
@@ -18,6 +18,18 @@
 weight_decay = 0.1
 adam_eps = 1e-08
 masked_score = -1e30
+
+
+def collect(x, axis, dim):
+    ways, here = (lax.axis_size(axis), lax.axis_index(axis))
+    grown, reach = (x, 1)
+    while reach < ways:
+        theirs = lax.ppermute(grown, axis, [(d, d ^ reach) for d in range(ways)])
+        mine_first = jnp.concatenate([grown, theirs], axis=dim)
+        theirs_first = jnp.concatenate([theirs, grown], axis=dim)
+        grown = jnp.where(here & reach == 0, mine_first, theirs_first)
+        reach = 2 * reach
+    return grown
 
 
 def split_weights(attn_flat, ffn_flat):
@@ -107,7 +119,7 @@
     groups = H // KV
     score_scale = HD ** (-0.5)
     attn_flat, ffn_flat = (
-        lax.all_gather(attn_master.astype(jnp.bfloat16), "seq", axis=0, tiled=True),
+        collect(attn_master.astype(jnp.bfloat16), "seq", 0),
         lax.all_gather(ffn_master.astype(jnp.bfloat16), "seq", axis=0, tiled=True),
     )
     gain_one, gain_two, bias_qkv, w_qkv, w_out, w_gu, w_down = split_weights(attn_flat, ffn_flat)

time: 1700 us -> 1640 us (0.965)
  other arithmetic: 304 us -> 242 us
    all_gather x1 -> x0, other arithmetic: 79.1 us -> none  [per_device(): lax.all_gather(attn_master.astype(jnp.bfloat16), 'seq', axis=0, tiled=True)]
    ppermute x0 -> x3, waiting for transfers between devices: none -> 59.7 us  [collect(): theirs = lax.ppermute(grown, axis, [(d, d ^ reach) for d in range(ways)])]
    all_gather x1 -> x0, waiting for transfers between devices: 50.1 us -> none  [per_device(): lax.all_gather(attn_master.astype(jnp.bfloat16), 'seq', axis=0, tiled=True)]
    select_n x0 -> x3, other arithmetic: none -> 18.4 us  [collect(): grown = jnp.where(here & reach == 0, mine_first, theirs_first)]
    unnamed x9 -> x8, waiting for transfers between devices: 356 us -> 357 us
  transfers between devices with their start and end apart: 8 -> 10, of which waited for: 4 -> 6; matrix products, arithmetic and copies ran while one was open for 23% -> 24% of each run, Pallas kernels for 0% -> 0%
where the time goes in v1:
time: 1640 us; the launch traced here: 1630 us
  waiting for transfers between devices  549 us (33%)
  matrix products  548 us (33%)
  local copies, waits for them, and re-layouts  255 us (16%)
  other arithmetic  242 us (15%)
  between operations  16.7 us (1%)
    unnamed x8, waiting for transfers between devices  357 us
    psum x1, waiting for transfers between devices, per_device(): lax.psum(attn_owned.astype(jnp.bfloat16), 'dp').astype(jnp.float32)  121 us
    dot_general x3, matrix products, delta_pass(): jnp.einsum('sckgd,sbkd->skgcb', grad_mixed, value_block, preferred_elemen...  98.9 us
    convert_element_type x1, other arithmetic, grad_pass(): (soft_prob * (grad_prob - row_delta[..., None])).astype(jnp.bfloat16)  92.1 us
    unnamed x156, local copies, waits for them, and re-layouts  78.9 us
    dot_general x4, matrix products, second_pass(): jnp.einsum('skgcb,sbkd->sckgd', soft_prob, value_block, preferred_element...  63.2 us
    ppermute x3, waiting for transfers between devices, collect(): theirs = lax.ppermute(grown, axis, [(d, d ^ reach) for d in range(ways)])  59.7 us
    dot_general x4, matrix products, block_scores(): jnp.einsum('sckgd,sbkd->skgcb', queries, key_block, preferred_element_typ...  55.2 us
  transfers between devices with their start and end apart: 10, of which 6 were waited for; matrix products, arithmetic and copies ran while one was open for 24% of the time, Pallas kernels for 0%

profile of v1, /device:TPU:0, one launch (start us, length us, event | category | flops | bytes accessed | tf_op | source)
XLA Modules:
  0.0 1625.3 jit_solution(15743590227834319081)
XLA Ops:
  13.7 20.8 %collective-permute-done.1 = bf16[459520]{0:T(1024)(128)(2,1)} collective-permute-done((bf16[459520]{0:T(1024)(128)(2,1)S(1)}, bf16[459520]{0:T(1024)(128)(2,1)}, u32[]{:S(2)}, u32[]{:S(2)}) %collective-permute-start.1) | collective-permute-done | bytes 919072 | tf_op jit(solution)/shard_map/ppermute | solution.py:27
  41.1 37.4 %collective-permute-done.2 = bf16[919040]{0:T(1024)(128)(2,1)} collective-permute-done((bf16[919040]{0:T(1024)(128)(2,1)S(1)}, bf16[919040]{0:T(1024)(128)(2,1)}, u32[]{:S(2)}, u32[]{:S(2)}) %collective-permute-start.2) | collective-permute-done | bytes 1838112 | tf_op jit(solution)/shard_map/ppermute | solution.py:27
  78.5 15.8 maximum_select_fusion
  115.8 8.8 all_gather.13
  155.8 11.8 all-gather.6.cloned.1.call-done
  170.1 15.9 fusion.20
  186.1 11.8 fusion.21
  197.9 11.8 fusion.19
  209.7 15.7 fusion.18
  225.4 17.7 %exponential_reduce_fusion = f32[4,2,7,256]{3,2,1,0:T(8,128)S(1)} fusion(f32[4,2,512,256,7]{3,2,4,1,0:T(8,128)} %get-tuple-element.80, f32[4,2,7,256]{3,2,1,0:T(8,128)S(1)} %get-tuple-element.30, pred[4,256,512]{1,2,0:T(8,128)(4,1)S(1)} %get-tuple-element.72), kind=kLoop, calls=%fused_computation.30 | loop fusion | flops 29345792 | bytes 29999104 | tf_op jit(solution)/shard_map/reduce_sum | solution.py:187
  250.1 13.2 exponential_reduce_fusion.2
  263.3 13.2 exponential_reduce_fusion.3
  276.6 15.2 fusion.54
  291.8 15.3 fusion.60
  307.2 14.8 fusion.57
  322.0 17.9 %add_convert_fusion.1 = bf16[4,2,64,7,256]{4,2,3,1,0:T(8,128)(2,1)} fusion(f32[4,2,64,7,256]{4,2,3,1,0:T(8,128)} %fusion.54, f32[4,2,64,7,256]{4,2,3,1,0:T(8,128)} %fusion.60, f32[4,2,64,7,256]{4,2,3,1,0:T(8,128)} %fusion.57, bf16[4,512,2,64,1]{1,3,4,2,0:T(8,128)(2,1)S(1)} %bitcast.284, f32[4,2,512,256,7]{3,2,4,1,0:T(8,128)} %get-tuple-element.80, ...), kind=kOutput, calls=%fused_computation.82 | convolution fusion | flops 972554240 | bytes 43311104 | tf_op jit(solution)/shard_map/skgcb,sbkd->sckgd/dot_general | solution.py:201
  346.8 12.5 slice.207
  359.3 29.8 %reshape.464 = bf16[896,9728,1]{1,0,2:T(8,128)(2,1)} reshape(bf16[8716288]{0:T(1024)(128)(2,1)} %slice.207) | data formatting | bytes 34865152 | tf_op jit(solution)/shard_map/slice | solution.py:44
  397.8 16.4 %reshape.465 = bf16[4864,896,1]{1,0,2:T(8,128)(2,1)} reshape(bf16[4358144]{0:T(1024)(128)(2,1)} %slice.210) | data formatting | bytes 17432576 | tf_op jit(solution)/shard_map/slice | solution.py:45
  414.2 30.3 %fusion.50 = f32[4,256,9728]{2,1,0:T(8,128)} fusion(bf16[896,9728,1]{1,0,2:T(8,128)(2,1)} %reshape.464, f32[4,256,896]{2,1,0:T(8,128)} %get-tuple-element.88, f32[896]{0:T(1024)S(1)} %copy-done.61, f32[4,256]{1,0:T(4,128)S(1)} %get-tuple-element.68), kind=kOutput, calls=%fused_computation.128 | convolution fusion | flops 17853710336 | bytes 60956160 | tf_op jit(solution)/shard_map/scd,df->scf/dot_general | solution.py:212
  444.5 30.6 %multiply_convert_fusion.1 = (bf16[4,256,4864]{2,1,0:T(8,128)(2,1)}, bf16[4,256,4864]{2,1,0:T(8,128)(2,1)}, bf16[4,256,4864]{2,1,0:T(8,128)(2,1)}) fusion(f32[4,256,9728]{2,1,0:T(8,128)} %fusion.50, bf16[4,256,896]{2,1,0:T(8,128)(2,1)S(1)} %copy-done.49, bf16[4864,896,1]{1,0,2:T(8,128)(2,1)} %reshape.465), kind=kOutput, calls=%fused_computation.41 | convolution fusion | flops 9000189952 | bytes 80281600 | tf_op jit(solution)/shard_map/scd,fd->scf/dot_general | solution.py:222
  475.1 30.4 %multiply_reduce_fusion = (f32[896]{0:T(1024)}, f32[4,256]{1,0:T(4,128)S(1)}, f32[4,256,896]{2,1,0:T(8,128)}) fusion(f32[4,256,896]{2,1,0:T(8,128)} %get-tuple-element.88, f32[4,256]{1,0:T(4,128)S(1)} %get-tuple-element.68, f32[896]{0:T(1024)S(1)} %copy-done.61, bf16[896,9728,1]{1,0,2:T(8,128)(2,1)} %reshape.464, ...), kind=kOutput, calls=%fused_computation.75 | convolution fusion | flops 17896308736 | bytes 44710912 | tf_op jit(solution)/shard_map/scf,df->scd/dot_general | solution.py:227
  516.9 13.8 fusion.46
  530.7 13.6 fusion.45
  544.3 13.6 fusion.44
  557.9 13.9 fusion.43
  571.9 11.6 fusion.93
  583.5 11.7 fusion.94
  595.1 11.7 fusion.95
  606.8 27.3 %convolution_bitcast_fusion = f32[896,9728]{1,0:T(8,128)} fusion(bf16[4,256,4864]{2,1,0:T(8,128)(2,1)} %get-tuple-element.34, bf16[4,256,4864]{2,1,0:T(8,128)(2,1)} %get-tuple-element.33, f32[4,256,896]{2,1,0:T(8,128)S(1)} %copy-done.33, f32[896]{0:T(1024)S(1)} %copy-done.61, f32[4,256]{1,0:T(4,128)S(1)} %get-tuple-element.68), kind=kOutput, calls=%fused_computation.38 | convolution fusion | flops 17893556224 | bytes 58465792 | tf_op jit(solution)/shard_map/scd,scf->df/dot_general | solution.py:226
  642.3 75.6 %fusion.7 = (f32[4,2,7,256]{3,2,1,0:T(8,128)}, f32[4,2,7,256]{3,2,1,0:T(8,128)}, f32[4,2,7,256]{3,2,1,0:T(8,128)}, f32[4,2,7,256]{3,2,1,0:T(8,128)}, f32[4,2,512,256,7]{3,2,4,1,0:T(8,128)}) fusion(f32[4,2,512,256,7]{3,2,4,1,0:T(8,128)} %get-tuple-element.84, f32[4,2,7,256]{3,2,1,0:T(8,128)S(1)} %copy-done.52, pred[4,256,512]{1,2,0:T(8,128)(4,1)S(1)} %copy-done.10, ...), kind=kOutput, calls=%fused_computation.14 | convolution fusion | flops 1086267392 | bytes 239624192 | tf_op jit(solution)/shard_map/sckgd,sbkd->skgcb/dot_general | solution.py:244
  718.8 92.1 %fusion.12 = (bf16[4,2,7,256,512]{3,4,2,1,0:T(8,128)(2,1)}, bf16[4,2,7,256,512]{3,4,2,1,0:T(8,128)(2,1)}, bf16[4,2,7,256,512]{3,4,2,1,0:T(8,128)(2,1)}, bf16[4,2,7,256,512]{3,4,2,1,0:T(8,128)(2,1)}) fusion(f32[4,2,512,256,7]{3,2,4,1,0:T(8,128)} %fusion.93, f32[4,2,512,256,7]{3,2,4,1,0:T(8,128)} %get-tuple-element.86, f32[4,2,7,256]{3,2,1,0:T(8,128)S(1)} %add_add_fusion, ...), kind=kLoop, calls=%fused_computation.21 | loop fusion | flops 176160768 | bytes 295813120 | tf_op jit(solution)/shard_map/convert_element_type | solution.py:263
  810.9 9.7 fusion.42
  820.6 9.7 fusion.41
  830.3 9.7 fusion.40
  840.0 10.5 fusion.39
  853.2 17.5 %convolution_bitcast_fusion.1 = f32[4864,896]{1,0:T(8,128)} fusion(bf16[4,256,4864]{2,1,0:T(8,128)(2,1)} %get-tuple-element.35, bf16[4,256,896]{2,1,0:T(8,128)(2,1)} %param.11), kind=kOutput, calls=%fused_computation.50 | convolution fusion | flops 8925478912 | bytes 29229056 | tf_op jit(solution)/shard_map/scf,scd->fd/dot_general | solution.py:221
  870.7 18.6 %reshape.451 = f32[4358144]{0:T(1024)} reshape(f32[4864,896]{1,0:T(8,128)} %convolution_bitcast_fusion.1) | data formatting | bytes 34865152 | tf_op jit(solution)/shard_map/reshape | solution.py:230
  889.3 33.4 %reshape.450 = f32[8716288]{0:T(1024)} reshape(f32[896,9728]{1,0:T(8,128)} %convolution_bitcast_fusion) | data formatting | bytes 69730304 | tf_op jit(solution)/shard_map/reshape | solution.py:230
  924.2 9.7 fusion.98
  933.9 9.6 fusion.96
  943.6 27.8 %fusion = bf16[13074432]{0:T(1024)(128)(2,1)} fusion(f32[4358144]{0:T(1024)} %reshape.451, f32[8716288]{0:T(1024)} %reshape.450), kind=kLoop, calls=%fused_computation.1 | loop fusion | flops 39223296 | bytes 78446592 | tf_op jit(solution)/shard_map/convert_element_type | solution.py:330
  1026.9 36.1 %dynamic-update-slice.3 = f32[1838080]{0:T(1024)} dynamic-update-slice(f32[1838080]{0:T(1024)} %constant_dynamic-update-slice_fusion.1, f32[1032192]{0:T(1024)} %reshape.448, s32[]{} %constant.88) | dynamic-update-slice | bytes 8257540
  1063.0 26.7 %dynamic-update-slice.4 = f32[1838080]{0:T(1024)} dynamic-update-slice(f32[1838080]{0:T(1024)} %dynamic-update-slice.3, f32[802816]{0:T(1024)S(1)} %reshape.449, s32[]{} %constant.89) | dynamic-update-slice | bytes 6422532
  1098.2 356.4 %all-reduce.7.cloned.1.call-done = (bf16[1838080]{0:T(1024)(128)(2,1)}, bf16[13074432]{0:T(1024)(128)(2,1)}) async-done(((bf16[1838080]{0:T(1024)(128)(2,1)}, bf16[13074432]{0:T(1024)(128)(2,1)}), (bf16[1838080]{0:T(1024)(128)(2,1)}, bf16[13074432]{0:T(1024)(128)(2,1)})) %all-reduce.7.cloned.1.call-update) | async-done | bytes 29825040
  1460.1 17.4 %add_convert_fusion = bf16[4,256,896]{2,1,0:T(8,128)(2,1)} fusion(f32[4,256,896]{2,1,0:T(8,128)} %get-tuple-element.88, bf16[4,256,4864]{2,1,0:T(8,128)(2,1)} %get-tuple-element.35, bf16[4864,896,1]{1,0,2:T(8,128)(2,1)} %reshape.465), kind=kOutput, calls=%fused_computation.79 | convolution fusion | flops 8927313920 | bytes 24182784 | tf_op jit(solution)/shard_map/scf,fd->scd/dot_general | solution.py:219
  1479.8 120.7 %all-reduce.9.cloned.1.call-done = (bf16[229760]{0:T(1024)(128)(2,1)}, bf16[1634304]{0:T(1024)(128)(2,1)}) async-done(((bf16[229760]{0:T(1024)(128)(2,1)}, bf16[1634304]{0:T(1024)(128)(2,1)}), (bf16[229760]{0:T(1024)(128)(2,1)}, bf16[1634304]{0:T(1024)(128)(2,1)})) %all-reduce.9.cloned.1.call-update) | async-done | bytes 3728144 | tf_op jit(solution)/shard_map/psum | solution.py:334
  1603.7 14.3 add_multiply_fusion
  (252 shorter events, 188.7 us)
Async XLA Ops:
  7.2 136.8 %all-gather.4.cloned.1.call-start = ((), (), s32[]{:S(2)}) async-start(), calls=%async_computation.2 | async-start | bytes 2359296 | tf_op jit(solution)/shard_map/all_gather | solution.py:147
  8.5 2.0 collective-permute-start
  10.8 23.7 %collective-permute-start.1 = (bf16[459520]{0:T(1024)(128)(2,1)S(1)}, bf16[459520]{0:T(1024)(128)(2,1)}, u32[]{:S(2)}, u32[]{:S(2)}) collective-permute-start(bf16[459520]{0:T(1024)(128)(2,1)S(1)} %maximum_select_fusion.2), channel_id=1, source_target_pairs={{0,2},{1,3},{2,0},{3,1},{4,6},{5,7},{6,4},{7,5},{8,10},{9,11},{10,... | collective-permute-start | bytes 2757128 | tf_op jit(solution)/shard_map/ppermute | solution.py:27
  36.7 41.8 %collective-permute-start.2 = (bf16[919040]{0:T(1024)(128)(2,1)S(1)}, bf16[919040]{0:T(1024)(128)(2,1)}, u32[]{:S(2)}, u32[]{:S(2)}) collective-permute-start(bf16[919040]{0:T(1024)(128)(2,1)S(1)} %maximum_select_fusion.1), channel_id=1, source_target_pairs={{0,4},{1,5},{2,6},{3,7},{4,0},{5,1},{6,2},{7,3},{8,12},{9,13},{10,... | collective-permute-start | bytes 5514248 | tf_op jit(solution)/shard_map/ppermute | solution.py:27
  41.1 59.0 %copy-start.57 = (f32[4,256]{1,0:T(4,128)}, f32[4,256]{1,0:T(4,128)S(1)}, u32[]{:S(2)}) copy-start(f32[4,256]{1,0:T(4,128)S(1)} %get-tuple-element.66) | copy-start | bytes 12292
  108.2 59.4 %all-gather.6.cloned.1.call-start = ((), (), s32[]{:S(2)}) async-start(), calls=%async_computation.3 | async-start | bytes 2359296 | tf_op jit(solution)/shard_map/all_gather | solution.py:146
  109.2 32.1 %copy-start.35 = (f32[4,256,32]{1,2,0:T(8,128)}, f32[4,256,32]{1,2,0:T(8,128)S(1)}, u32[]{:S(2)}) copy-start(f32[4,256,32]{1,2,0:T(8,128)S(1)} %get-tuple-element.63) | copy-start | bytes 393220
  109.2 32.1 %copy-start.37 = (f32[4,256,32]{1,2,0:T(8,128)}, f32[4,256,32]{1,2,0:T(8,128)S(1)}, u32[]{:S(2)}) copy-start(f32[4,256,32]{1,2,0:T(8,128)S(1)} %get-tuple-element.64) | copy-start | bytes 393220
  111.4 235.3 %all-gather.8.cloned.1.call-start = ((), (), s32[]{:S(2)}) async-start(), calls=%async_computation.4 | async-start | bytes 29417472 | tf_op jit(solution)/shard_map/all_gather | solution.py:123
  115.8 884.3 %reduce-scatter.3.cloned.1.call-start = ((), (), s32[]{:S(2)}) async-start(), calls=%async_computation.5 | async-start | bytes 2359296 | tf_op jit(solution)/shard_map/reduce_scatter | solution.py:293
  127.8 70.0 %copy-start.8 = (pred[4,256,512]{1,2,0:T(8,128)(4,1)}, pred[4,256,512]{1,2,0:T(8,128)(4,1)S(1)}, u32[]{:S(2)}) copy-start(pred[4,256,512]{1,2,0:T(8,128)(4,1)S(1)} %get-tuple-element.70) | copy-start | bytes 1572868
  127.8 194.1 %copy-start.4 = (pred[4,256,512]{1,2,0:T(8,128)(4,1)}, pred[4,256,512]{1,2,0:T(8,128)(4,1)S(1)}, u32[]{:S(2)}) copy-start(pred[4,256,512]{1,2,0:T(8,128)(4,1)S(1)} %get-tuple-element.72) | copy-start | bytes 1572868
  144.0 65.7 %copy-start = (bf16[4,256,2,7,32]{1,4,3,2,0:T(8,128)(2,1)}, bf16[4,256,2,7,32]{1,4,3,2,0:T(8,128)(2,1)S(1)}, u32[]{:S(2)}) copy-start(bf16[4,256,2,7,32]{1,4,3,2,0:T(8,128)(2,1)S(1)} %get-tuple-element.38) | copy-start | bytes 2752516
  144.0 65.7 %copy-start.2 = (bf16[4,256,2,7,32]{1,4,3,2,0:T(8,128)(2,1)}, bf16[4,256,2,7,32]{1,4,3,2,0:T(8,128)(2,1)S(1)}, u32[]{:S(2)}) copy-start(bf16[4,256,2,7,32]{1,4,3,2,0:T(8,128)(2,1)S(1)} %get-tuple-element.39) | copy-start | bytes 2752516
  170.1 15.9 copy-start.23
  170.1 27.8 %copy-start.25 = (bf16[4,512,128]{1,2,0:T(8,128)(2,1)}, bf16[4,512,128]{1,2,0:T(8,128)(2,1)S(1)}, u32[]{:S(2)}) copy-start(bf16[4,512,128]{1,2,0:T(8,128)(2,1)S(1)} %get-tuple-element.49) | copy-start | bytes 1572868
  209.7 33.5 %slice-start = ((s8[29360128]{0:T(1024)(128)(4,1)}), s8[4194304]{0:T(1024)(128)(4,1)S(1)}, s32[]{:S(2)}) async-start(s8[29360128]{0:T(1024)(128)(4,1)} %bitcast.272), calls=%async_computation.9 | async-start | bytes 8388608
  209.7 33.5 %slice-start.1 = ((s8[29360128]{0:T(1024)(128)(4,1)}), s8[4194304]{0:T(1024)(128)(4,1)S(1)}, s32[]{:S(2)}) async-start(s8[29360128]{0:T(1024)(128)(4,1)} %bitcast.272), calls=%async_computation.10 | async-start | bytes 8388608
  209.7 33.5 %slice-start.2 = ((s8[29360128]{0:T(1024)(128)(4,1)}), s8[4194304]{0:T(1024)(128)(4,1)S(1)}, s32[]{:S(2)}) async-start(s8[29360128]{0:T(1024)(128)(4,1)} %bitcast.272), calls=%async_computation.11 | async-start | bytes 8388608
  209.7 33.5 %slice-start.3 = ((s8[29360128]{0:T(1024)(128)(4,1)}), s8[4194304]{0:T(1024)(128)(4,1)S(1)}, s32[]{:S(2)}) async-start(s8[29360128]{0:T(1024)(128)(4,1)} %bitcast.272), calls=%async_computation.12 | async-start | bytes 8388608
  225.4 17.8 %slice-start.4 = ((s8[29360128]{0:T(1024)(128)(4,1)}), s8[4194304]{0:T(1024)(128)(4,1)S(1)}, s32[]{:S(2)}) async-start(s8[29360128]{0:T(1024)(128)(4,1)} %bitcast.272), calls=%async_computation.13 | async-start | bytes 8388608
  225.4 17.8 %slice-start.5 = ((s8[29360128]{0:T(1024)(128)(4,1)}), s8[4194304]{0:T(1024)(128)(4,1)S(1)}, s32[]{:S(2)}) async-start(s8[29360128]{0:T(1024)(128)(4,1)} %bitcast.272), calls=%async_computation.14 | async-start | bytes 8388608
  225.4 17.8 %slice-start.6 = ((s8[29360128]{0:T(1024)(128)(4,1)}), s8[4194304]{0:T(1024)(128)(4,1)S(1)}, s32[]{:S(2)}) async-start(s8[29360128]{0:T(1024)(128)(4,1)} %bitcast.272), calls=%async_computation.15 | async-start | bytes 8388608
  225.4 17.8 %copy-start.11 = (pred[4,256,512]{1,2,0:T(8,128)(4,1)S(1)}, pred[4,256,512]{1,2,0:T(8,128)(4,1)}, u32[]{:S(2)}) copy-start(pred[4,256,512]{1,2,0:T(8,128)(4,1)} %get-tuple-element.71) | copy-start | bytes 1572868
  276.6 45.4 %copy-start.51 = (f32[4,2,7,256]{3,2,1,0:T(8,128)}, f32[4,2,7,256]{3,2,1,0:T(8,128)S(1)}, u32[]{:S(2)}) copy-start(f32[4,2,7,256]{3,2,1,0:T(8,128)S(1)} %log_add_fusion) | copy-start | bytes 172036
  322.0 17.9 %copy-start.18 = (bf16[4,256,896]{2,1,0:T(8,128)(2,1)S(1)}, bf16[4,256,896]{2,1,0:T(8,128)(2,1)}, u32[]{:S(2)}) copy-start(bf16[4,256,896]{2,1,0:T(8,128)(2,1)} %param.10) | copy-start | bytes 5505028
  397.8 16.4 %copy-start.61 = (f32[896]{0:T(1024)S(1)}, f32[896]{0:T(1024)}, u32[]{:S(2)}) copy-start(f32[896]{0:T(1024)} %get-tuple-element.40) | copy-start | bytes 10756
  414.2 30.3 %copy-start.49 = (bf16[4,256,896]{2,1,0:T(8,128)(2,1)S(1)}, bf16[4,256,896]{2,1,0:T(8,128)(2,1)}, u32[]{:S(2)}) copy-start(bf16[4,256,896]{2,1,0:T(8,128)(2,1)} %param.11) | copy-start | bytes 5505028
  475.1 30.4 %copy-start.32 = (f32[4,256,896]{2,1,0:T(8,128)S(1)}, f32[4,256,896]{2,1,0:T(8,128)}, u32[]{:S(2)}) copy-start(f32[4,256,896]{2,1,0:T(8,128)} %get-tuple-element.88) | copy-start | bytes 11010052
  475.1 30.4 %copy-start.62 = (f32[4,256]{1,0:T(4,128)S(1)}, f32[4,256]{1,0:T(4,128)}, u32[]{:S(2)}) copy-start(f32[4,256]{1,0:T(4,128)} %get-tuple-element.67) | copy-start | bytes 12292
  718.8 92.1 %copy-start.1 = (bf16[4,256,2,7,32]{1,4,3,2,0:T(8,128)(2,1)S(1)}, bf16[4,256,2,7,32]{1,4,3,2,0:T(8,128)(2,1)}, u32[]{:S(2)}) copy-start(bf16[4,256,2,7,32]{1,4,3,2,0:T(8,128)(2,1)} %copy-done) | copy-start | bytes 2752516
  718.8 92.1 %copy-start.3 = (bf16[4,256,2,7,32]{1,4,3,2,0:T(8,128)(2,1)S(1)}, bf16[4,256,2,7,32]{1,4,3,2,0:T(8,128)(2,1)}, u32[]{:S(2)}) copy-start(bf16[4,256,2,7,32]{1,4,3,2,0:T(8,128)(2,1)} %copy-done.2) | copy-start | bytes 2752516
  853.2 149.8 %reduce-scatter.5.cloned.1.call-start = ((), (), s32[]{:S(2)}) async-start(), calls=%async_computation.6 | async-start | bytes 2359296 | tf_op jit(solution)/shard_map/reduce_scatter | solution.py:296
  889.3 33.4 %copy-start.45 = (bf16[4,512,128]{2,1,0:T(8,128)(2,1)S(1)}, bf16[4,512,128]{2,1,0:T(8,128)(2,1)}, u32[]{:S(2)}) copy-start(bf16[4,512,128]{2,1,0:T(8,128)(2,1)} %copy.127) | copy-start | bytes 1572868
  889.3 33.4 %copy-start.46 = (bf16[4,512,128]{2,1,0:T(8,128)(2,1)S(1)}, bf16[4,512,128]{2,1,0:T(8,128)(2,1)}, u32[]{:S(2)}) copy-start(bf16[4,512,128]{2,1,0:T(8,128)(2,1)} %copy.126) | copy-start | bytes 1572868
  889.3 33.4 %copy-start.47 = (bf16[4,512,128]{2,1,0:T(8,128)(2,1)S(1)}, bf16[4,512,128]{2,1,0:T(8,128)(2,1)}, u32[]{:S(2)}) copy-start(bf16[4,512,128]{2,1,0:T(8,128)(2,1)} %copy.125) | copy-start | bytes 1572868
  889.3 33.4 %copy-start.48 = (bf16[4,512,128]{2,1,0:T(8,128)(2,1)S(1)}, bf16[4,512,128]{2,1,0:T(8,128)(2,1)}, u32[]{:S(2)}) copy-start(bf16[4,512,128]{2,1,0:T(8,128)(2,1)} %copy.124) | copy-start | bytes 1572868
  889.3 34.9 %copy-start.29 = (bf16[4,512,128]{1,2,0:T(8,128)(2,1)S(1)}, bf16[4,512,128]{1,2,0:T(8,128)(2,1)}, u32[]{:S(2)}) copy-start(bf16[4,512,128]{1,2,0:T(8,128)(2,1)} %copy-done.28) | copy-start | bytes 1572868
  943.6 27.9 %copy-start.26 = (bf16[4,512,128]{1,2,0:T(8,128)(2,1)S(1)}, bf16[4,512,128]{1,2,0:T(8,128)(2,1)}, u32[]{:S(2)}) copy-start(bf16[4,512,128]{1,2,0:T(8,128)(2,1)} %copy-done.25) | copy-start | bytes 1572868
  943.6 511.1 %all-reduce.7.cloned.1.call-start = ((), (), s32[]{:S(2)}) async-start(), calls=%async_computation.7 | async-start | bytes 59650048
  1095.7 504.8 %all-reduce.9.cloned.1.call-start = ((), (), s32[]{:S(2)}) async-start(), calls=%async_computation.8 | async-start | bytes 7458816 | tf_op jit(solution)/shard_map/psum | solution.py:334
  1460.0 17.4 %copy-start.17 = (f32[4,256,896]{2,1,0:T(8,128)S(1)}, f32[4,256,896]{2,1,0:T(8,128)}, u32[]{:S(2)}) copy-start(f32[4,256,896]{2,1,0:T(8,128)} %copy-done.16) | copy-start | bytes 11010052
  1460.0 17.4 %copy-start.19 = (bf16[4,256,896]{2,1,0:T(8,128)(2,1)S(1)}, bf16[4,256,896]{2,1,0:T(8,128)(2,1)}, u32[]{:S(2)}) copy-start(bf16[4,256,896]{2,1,0:T(8,128)(2,1)} %param.10) | copy-start | bytes 5505028
  1460.0 17.4 %copy-start.34 = (f32[4,256,896]{2,1,0:T(8,128)S(1)}, f32[4,256,896]{2,1,0:T(8,128)}, u32[]{:S(2)}) copy-start(f32[4,256,896]{2,1,0:T(8,128)} %get-tuple-element.91) | copy-start | bytes 11010052
  1460.0 17.4 %copy-start.56 = (f32[4,256]{1,0:T(4,128)S(1)}, f32[4,256]{1,0:T(4,128)}, u32[]{:S(2)}) copy-start(f32[4,256]{1,0:T(4,128)} %get-tuple-element.65) | copy-start | bytes 12292
  1477.4 123.1 %copy-start.31 = (f32[229760]{0:T(1024)S(1)}, f32[229760]{0:T(1024)}, u32[]{:S(2)}) copy-start(f32[229760]{0:T(1024)} %param.14) | copy-start | bytes 2757124
  1477.4 123.1 %copy-start.53 = (f32[229760]{0:T(1024)S(1)}, f32[229760]{0:T(1024)}, u32[]{:S(2)}) copy-start(f32[229760]{0:T(1024)} %param.15) | copy-start | bytes 2757124
  1477.4 123.1 %copy-start.54 = (f32[229760]{0:T(1024)S(1)}, f32[229760]{0:T(1024)}, u32[]{:S(2)}) copy-start(f32[229760]{0:T(1024)} %param.16) | copy-start | bytes 2757124
  (36 other events, 324.7 us)
Sparse Core Ops, SparseCore 0:
  108.3 29.1 all-gather.3
  139.4 28.1 all-gather.5
  170.0 129.4 all-gather.7
  853.3 41.1 reduce-scatter.2
  943.7 41.2 reduce-scatter.4
  1095.9 358.7 all-reduce.6
  1460.1 140.3 all-reduce.8
